TPU v7x, 32 devices: a whole 2x2x4 slice. The times are simulated.
32 devices in a mesh: tm: 4 (over x, core), space: 8 (over z, y).
Axes of the slice: x: 2, y: 2, z: 4, core: 2. Of those that a mesh axis runs over, the one named last changes fastest.
Arguments:
- starts: float32 [4, 4, 64, 8192], P('tm', None, 'space'), may hold values from -6 to 6
- labels: int32 [64, 8192], P('space'), may hold values from 0 to 3
- coef_table: float32 [3, 4], replicated, may hold values from 0.2 to 1.2
Outputs:
- new_starts: float32 [4, 4, 64, 8192], P('tm', None, 'space')
All inputs are finite; a program needn't handle non-finite values.
Results may differ from a plain program's by a relative error of at most 0.00015.
Values sent between devices are 32-bit elements; how exact they have to be, the bound alone decides.
A program may use at most 192 MiB of HBM per device.

v0:
```python
import jax
import jax.numpy as jnp
from jax import lax
from jax.sharding import PartitionSpec as P

NX = 32
FINE = 4


fine_tau = 0.1
coarse_tau = 0.4


def extended(cells, sides, width):
    for axis, dim in sides:
        count = lax.axis_size(axis)
        ends = count - 1
        head = lax.slice_in_dim(cells, 0, width, axis=dim)
        tail = lax.slice_in_dim(cells, cells.shape[dim] - width, cells.shape[dim], axis=dim)
        cells = jnp.concatenate(
            [
                lax.ppermute(tail, axis, [(i, (i + 1) % count) for i in range(ends)]),
                cells,
                lax.ppermute(head, axis, [((i + 1) % count, i) for i in range(ends)]),
            ],
            axis=dim,
        )
    return cells


def shifted(array, axis, by):
    size = lax.axis_size(axis)
    pairs = [(i, i + by) for i in range(size) if 0 <= i + by < size]
    return lax.ppermute(array, axis, pairs)


def lookup(labels, table):
    fields = jnp.zeros((3,) + labels.shape, jnp.float32)
    for tissue in range(table.shape[1]):
        chosen = (labels == tissue).astype(jnp.float32)
        fields = fields + table[:, tissue][:, None, None] * chosen[None]
    return fields


def shift_flat(field_in, offset):
    filler = jnp.zeros(field_in.shape[:-1] + (abs(offset),), field_in.dtype)
    if offset > 0:
        return jnp.concatenate([field_in[..., offset:], filler], -1)
    return jnp.concatenate([filler, field_in[..., :offset]], -1)


def biot_update(padded, coefficients, plane_width, tau, spacing):
    field_now = padded[:, 1:-1]
    components, z_depth, plane_cells = field_now.shape
    length = plane_cells // plane_width
    column = lax.broadcasted_iota(jnp.int32, (1, 1, plane_cells), 2) % length
    x_up = shift_flat(field_now, length)
    x_dn = shift_flat(field_now, -length)
    y_up = jnp.where(column != length - 1, shift_flat(field_now, 1), 0.0)
    y_dn = jnp.where(column != 0, shift_flat(field_now, -1), 0.0)
    z_up = padded[:, 2:]
    z_dn = padded[:, :-2]
    laplacian = (x_up + x_dn + y_up + y_dn + z_up + z_dn - 6.0 * field_now) / (spacing * spacing)
    inv_two = 1.0 / (2.0 * spacing)
    grad_x = (x_up[3] - x_dn[3]) * inv_two
    grad_y = (y_up[3] - y_dn[3]) * inv_two
    grad_z = (z_up[3] - z_dn[3]) * inv_two
    divergence = (x_up[0] - x_dn[0] + y_up[1] - y_dn[1] + z_up[2] - z_dn[2]) * inv_two
    shear_field = coefficients[0]
    perm_field = coefficients[1]
    couple_field = coefficients[2]
    shifted_disp = field_now[:3] + tau * (
        shear_field * laplacian[:3] - couple_field * jnp.stack([grad_x, grad_y, grad_z])
    )
    pressure = field_now[3] + tau * (perm_field * laplacian[3] - couple_field * divergence)
    return jnp.concatenate([shifted_disp, pressure[None]], 0)


def restrict(field_in, plane_width):
    components, z_depth, plane_cells = field_in.shape
    length = plane_cells // plane_width
    blocks = field_in.reshape(components, z_depth // 2, 2, plane_width // 2, 2, length // 2, 2)
    return blocks.sum(axis=(2, 4, 6)).reshape(components, z_depth // 2, -1) * 0.125


def prolong(field_in, plane_width):
    components, z_depth, plane_cells = field_in.shape
    length = plane_cells // plane_width
    shaped = field_in.reshape(components, z_depth, 1, plane_width, 1, length, 1)
    spread = jnp.broadcast_to(shaped, (components, z_depth, 2, plane_width, 2, length, 2))
    return spread.reshape(components, 2 * z_depth, 4 * plane_cells)


def substitute(factor, right_side):
    order = factor.shape[0]
    forward = []
    for row_index in range(order):
        running = right_side[row_index]
        for column in range(row_index):
            running = running - factor[row_index, column] * forward[column]
        forward.append(running / factor[row_index, row_index])
    backward = [None] * order
    for row_index in reversed(range(order)):
        running = forward[row_index]
        for column in range(row_index + 1, order):
            running = running - factor[column, row_index] * backward[column]
        backward[row_index] = running / factor[row_index, row_index]
    return jnp.stack(backward)


def solve_weights(defect, flat_ru, factor):
    partial_value = jnp.dot(flat_ru, defect.reshape(-1), precision=lax.Precision.HIGHEST)
    inner_products = lax.psum(partial_value, "space")
    return substitute(factor, inner_products)


def coarse_image(field_in, coarse_coefs, plane_width):
    padded = extended(field_in, (("space", 1),), 1)
    return biot_update(padded, coarse_coefs, plane_width, coarse_tau, 2.0)


def combine(weights, flat_basis, shape):
    return jnp.dot(weights, flat_basis, precision=lax.Precision.HIGHEST).reshape(shape)


def shards(starts, labels, coef_table):
    highest = lax.Precision.HIGHEST
    coarse_width = NX // 2
    coefficients = lookup(labels, coef_table)
    coarse_coefs = restrict(coefficients, NX)
    field_now = starts[0]
    for fine_step in range(FINE):
        padded = extended(field_now, (("space", 1),), 1)
        field_now = biot_update(padded, coefficients, NX, fine_tau, 1.0)
    coarse_start = restrict(starts[0], NX)
    coarse_end = restrict(field_now, NX)
    all_ru, all_rf = (
        lax.all_gather(coarse_start[None], "tm", axis=0, tiled=True),
        lax.all_gather(coarse_end[None], "tm", axis=0, tiled=True),
    )
    slices = all_ru.shape[0]
    flat_ru = all_ru.reshape(slices, -1)
    flat_rf = all_rf.reshape(slices, -1)
    gram = lax.psum(jnp.dot(flat_ru, flat_ru.T, precision=highest), "space")
    factor = jnp.linalg.cholesky(gram)
    shape = coarse_start.shape

    def coarse_map(defect):
        weights = solve_weights(defect, flat_ru, factor)
        remainder = defect - combine(weights, flat_ru, shape)
        return coarse_image(remainder, coarse_coefs, coarse_width) + combine(
            weights, flat_rf, shape
        )

    tm_index = lax.axis_index("tm")
    zero_field = jnp.zeros_like(coarse_start)
    ru_next = lax.dynamic_index_in_dim(
        all_ru, jnp.minimum(tm_index + 1, slices - 1), 0, keepdims=False
    )

    def turn(turn_index, loop_carry):
        defect, own_update = loop_carry
        correction = coarse_map(defect)
        own_update = jnp.where(tm_index == turn_index, correction, own_update)
        outgoing = coarse_end + correction - ru_next
        defect = shifted(outgoing, "tm", 1)
        return (defect, own_update)

    final_carry = lax.fori_loop(0, slices, turn, (zero_field, zero_field))
    own_update = final_carry[1]
    return (field_now + prolong(own_update, coarse_width))[None]


def solution(mesh):
    placed = (P("tm", None, "space", None), P("space", None), P())
    return jax.shard_map(
        shards, mesh=mesh, in_specs=placed, out_specs=P("tm", None, "space", None), check_vma=False
    )
```

profile of v0, /device:TPU:1, one launch (start us, length us, event | category | flops | bytes accessed | tf_op | source)
XLA Modules:
  0.0 679.4 jit_solution(7649384507275400338)
XLA Ops:
  3.9 5.3 collective-permute-start.4
  13.5 15.5 %copy.42 = f32[1,4,8,8192]{1,3,2,0:T(8,128)} copy(f32[1,4,8,8192]{3,2,1,0:T(8,128)S(1)} %copy-done) | data formatting | bytes 2097152 | tf_op args[0]
  29.3 23.2 %mul.700 = f32[4,2,16,2,128,2]{5,4,3,2,1,0:T(8,128)} reshape(f32[8,8192]{1,0:T(8,128)S(1)} %get-tuple-element.437) | data formatting | bytes 524288 | tf_op jit(solution)/shard_map/mul | solution.py:41
  52.5 11.0 %copy.48 = f32[4,2,16,2,128,2]{4,2,5,3,1,0:T(8,128)} copy(f32[4,2,16,2,128,2]{5,4,3,2,1,0:T(8,128)} %mul.700) | data formatting | bytes 524288 | tf_op jit(solution)/shard_map/mul | solution.py:41
  63.5 23.1 %mul.704 = f32[4,2,16,2,128,2]{5,4,3,2,1,0:T(8,128)} reshape(f32[8,8192]{1,0:T(8,128)S(1)} %get-tuple-element.438) | data formatting | bytes 524288 | tf_op jit(solution)/shard_map/mul | solution.py:41
  86.7 10.7 %copy.49 = f32[4,2,16,2,128,2]{4,2,5,3,1,0:T(8,128)} copy(f32[4,2,16,2,128,2]{5,4,3,2,1,0:T(8,128)} %mul.704) | data formatting | bytes 524288 | tf_op jit(solution)/shard_map/mul | solution.py:41
  97.4 23.1 %mul.708 = f32[4,2,16,2,128,2]{5,4,3,2,1,0:T(8,128)} reshape(f32[8,8192]{1,0:T(8,128)S(1)} %get-tuple-element.440) | data formatting | bytes 524288 | tf_op jit(solution)/shard_map/mul | solution.py:41
  120.6 10.8 %copy.50 = f32[4,2,16,2,128,2]{4,2,5,3,1,0:T(8,128)} copy(f32[4,2,16,2,128,2]{5,4,3,2,1,0:T(8,128)} %mul.708) | data formatting | bytes 524288 | tf_op jit(solution)/shard_map/mul | solution.py:41
  131.4 23.1 %mul.712 = f32[4,2,16,2,128,2]{5,4,3,2,1,0:T(8,128)} reshape(f32[8,8192]{1,0:T(8,128)S(1)} %get-tuple-element.439) | data formatting | bytes 524288 | tf_op jit(solution)/shard_map/mul | solution.py:41
  154.5 10.6 %copy.51 = f32[4,2,16,2,128,2]{4,2,5,3,1,0:T(8,128)} copy(f32[4,2,16,2,128,2]{5,4,3,2,1,0:T(8,128)} %mul.712) | data formatting | bytes 524288 | tf_op jit(solution)/shard_map/mul | solution.py:41
  168.5 24.4 %reduce_sum.27 = f32[4,4,16,128]{0,3,2,1:T(8,128)} reduce(f32[4,4,2,16,2,128,2]{0,6,5,4,3,2,1:T(2,128)} %bitcast.116, f32[]{:T(128)} %constant.189.clone.1), dimensions={2,4,6}, to_apply=%region_0.0 | reduce | flops 229376 | bytes 1179652 | tf_op jit(solution)/shard_map/reduce_sum | solution.py:83
  192.9 4.9 broadcast_multiply_fusion.1
  200.6 8.9 %all_gather.6 = f32[4,4,4,2048]{3,2,1,0:T(4,128)S(1)} all-gather(f32[1,4,4,2048]{3,2,1,0:T(4,128)S(1)} %copy.43), channel_id=1, replica_groups=mesh['tm'=4,'space'=8] {'tm'}, dimensions={0}, use_global_device_ids=true | all-gather | bytes 655360 | tf_op jit(solution)/shard_map/all_gather | solution.py:138
  211.9 15.8 %psum.21 = f32[4,4]{0,1:T(4,128)S(1)} all-reduce(f32[4,4]{0,1:T(4,128)S(1)} %convolution_bitcast_fusion.1), channel_id=1, replica_groups=mesh['tm'=4,'space'=8] {'space'}, use_global_device_ids=true, to_apply=%region_1.2 | all-reduce | flops 16 | bytes 128 | tf_op jit(solution)/shard_map/psum | solution.py:144
  265.6 5.1 collective-permute-done.9
  272.3 69.4 %concatenate.185 = f32[3,4,2,16,2,128,2]{6,5,4,3,2,1,0:T(8,128)} reshape(f32[3,8,8192]{2,1,0:T(8,128)S(1)} %fusion.54) | data formatting | bytes 1572864 | tf_op jit(solution)/shard_map/concatenate | solution.py:76
  341.8 29.0 %copy.52 = f32[3,4,2,16,2,128,2]{5,3,6,4,2,1,0:T(8,128)S(1)} copy(f32[3,4,2,16,2,128,2]{6,5,4,3,2,1,0:T(8,128)} %concatenate.185) | data formatting | bytes 1572864 | tf_op jit(solution)/shard_map/concatenate | solution.py:76
  370.8 23.1 %concatenate.186 = f32[1,4,2,16,2,128,2]{6,5,4,3,2,1,0:T(8,128)} reshape(f32[1,8,8192]{2,1,0:T(8,128)S(1)} %get-tuple-element.394) | data formatting | bytes 524288 | tf_op jit(solution)/shard_map/concatenate | solution.py:76
  394.0 10.0 %copy.53 = f32[1,4,2,16,2,128,2]{5,3,6,4,2,1,0:T(8,128)S(1)} copy(f32[1,4,2,16,2,128,2]{6,5,4,3,2,1,0:T(8,128)} %concatenate.186) | data formatting | bytes 524288 | tf_op jit(solution)/shard_map/concatenate | solution.py:76
  406.7 4.7 broadcast_multiply_fusion
  414.3 14.3 %all_gather.7 = f32[4,4,4,2048]{3,2,1,0:T(4,128)S(1)} all-gather(f32[1,4,4,2048]{3,2,1,0:T(4,128)S(1)} %copy.55), channel_id=1, replica_groups=mesh['tm'=4,'space'=8] {'tm'}, dimensions={0}, use_global_device_ids=true | all-gather | bytes 655360 | tf_op jit(solution)/shard_map/all_gather | solution.py:139
  432.2 211.3 %while.18 = (s32[]{:T(128)}, f32[4,4,2048]{2,1,0:T(4,128)S(1)}, f32[4,4,2048]{2,1,0:T(4,128)S(1)}, f32[4,32768]{1,0:T(4,128)S(1)}, f32[4,4]{1,0:T(4,128)S(1)}, /...) while((s32[]{:T(128)}, f32[4,4,2048]{2,1,0:T(4,128)S(1)}, ...), condition=%wide.region_8.9_spmd.clone, body=%wide.region_6.8_spmd.clone.sunk | while | flops 5701683 | bytes 8692181 | solution.py:169
  435.4 16.3 %psum.24 = f32[4]{0:T(128)S(1)} all-reduce(f32[4]{0:T(128)S(1)} %convolution_bitcast_fusion.3), channel_id=1, replica_groups=mesh['tm'=4,'space'=8] {'space'}, use_global_device_ids=true, to_apply=%region_7.7 | all-reduce | flops 4 | bytes 32 | tf_op jit(solution)/shard_map/while/body/eval_jaxpr/psum | solution.py:113
  474.4 7.8 %collective-permute-start.2 = (f32[4,4,2048]{2,1,0:T(4,128)S(1)}, f32[4,4,2048]{2,1,0:T(4,128)S(1)}, u32[]{:S(2)}, u32[]{:S(2)}) collective-permute-start(f32[4,4,2048]{2,1,0:T(4,128)S(1)} %get-tuple-element.570), channel_id=1, source_target_pairs={{0,8},{8,16},{16,24},{1,9},{9,17},{17,25},{2,10},{10,18},{18,26},{... | collective-permute-start | bytes 393224 | tf_op jit(solution)/shard_map/while/body/eval_jaxpr/ppermute | solution.py:34
  487.4 15.2 %psum.24 = f32[4]{0:T(128)S(1)} all-reduce(f32[4]{0:T(128)S(1)} %convolution_bitcast_fusion.3), channel_id=1, replica_groups=mesh['tm'=4,'space'=8] {'space'}, use_global_device_ids=true, to_apply=%region_7.7 | all-reduce | flops 4 | bytes 32 | tf_op jit(solution)/shard_map/while/body/eval_jaxpr/psum | solution.py:113
  525.9 9.4 %collective-permute-start.2 = (f32[4,4,2048]{2,1,0:T(4,128)S(1)}, f32[4,4,2048]{2,1,0:T(4,128)S(1)}, u32[]{:S(2)}, u32[]{:S(2)}) collective-permute-start(f32[4,4,2048]{2,1,0:T(4,128)S(1)} %get-tuple-element.570), channel_id=1, source_target_pairs={{0,8},{8,16},{16,24},{1,9},{9,17},{17,25},{2,10},{10,18},{18,26},{... | collective-permute-start | bytes 393224 | tf_op jit(solution)/shard_map/while/body/eval_jaxpr/ppermute | solution.py:34
  540.5 14.3 %psum.24 = f32[4]{0:T(128)S(1)} all-reduce(f32[4]{0:T(128)S(1)} %convolution_bitcast_fusion.3), channel_id=1, replica_groups=mesh['tm'=4,'space'=8] {'space'}, use_global_device_ids=true, to_apply=%region_7.7 | all-reduce | flops 4 | bytes 32 | tf_op jit(solution)/shard_map/while/body/eval_jaxpr/psum | solution.py:113
  578.9 9.5 %collective-permute-start.2 = (f32[4,4,2048]{2,1,0:T(4,128)S(1)}, f32[4,4,2048]{2,1,0:T(4,128)S(1)}, u32[]{:S(2)}, u32[]{:S(2)}) collective-permute-start(f32[4,4,2048]{2,1,0:T(4,128)S(1)} %get-tuple-element.570), channel_id=1, source_target_pairs={{0,8},{8,16},{16,24},{1,9},{9,17},{17,25},{2,10},{10,18},{18,26},{... | collective-permute-start | bytes 393224 | tf_op jit(solution)/shard_map/while/body/eval_jaxpr/ppermute | solution.py:34
  593.6 14.3 %psum.24 = f32[4]{0:T(128)S(1)} all-reduce(f32[4]{0:T(128)S(1)} %convolution_bitcast_fusion.3), channel_id=1, replica_groups=mesh['tm'=4,'space'=8] {'space'}, use_global_device_ids=true, to_apply=%region_7.7 | all-reduce | flops 4 | bytes 32 | tf_op jit(solution)/shard_map/while/body/eval_jaxpr/psum | solution.py:113
  632.1 9.5 %collective-permute-start.2 = (f32[4,4,2048]{2,1,0:T(4,128)S(1)}, f32[4,4,2048]{2,1,0:T(4,128)S(1)}, u32[]{:S(2)}, u32[]{:S(2)}) collective-permute-start(f32[4,4,2048]{2,1,0:T(4,128)S(1)} %get-tuple-element.570), channel_id=1, source_target_pairs={{0,8},{8,16},{16,24},{1,9},{9,17},{17,25},{2,10},{10,18},{18,26},{... | collective-permute-start | bytes 393224 | tf_op jit(solution)/shard_map/while/body/eval_jaxpr/ppermute | solution.py:34
  646.3 13.4 %broadcast_in_dim.136 = f32[4,4,2,16,2,128,2]{0,6,5,4,3,2,1:T(2,128)} broadcast(f32[4,4,16,128]{0,3,2,1:T(8,128)} %bitcast.126), dimensions={0,1,3,5} | broadcast | bytes 1179648 | tf_op jit(solution)/shard_map/broadcast_in_dim | solution.py:90
  659.7 18.2 %copy.58 = f32[1,4,8,8192]{3,2,1,0:T(8,128)S(1)} copy(f32[1,4,8,8192]{1,3,2,0:T(8,128)} %bitcast.117) | data formatting | bytes 2097152 | tf_op jit(solution)/shard_map/reshape | solution.py:91
  (190 shorter events, 125.5 us)
Async XLA Ops:
  2.5 9.3 %copy-start = (f32[1,4,8,8192]{3,2,1,0:T(8,128)S(1)}, f32[1,4,8,8192]{3,2,1,0:T(8,128)}, u32[]{:S(2)}) copy-start(f32[1,4,8,8192]{3,2,1,0:T(8,128)} %param.5) | copy-start | bytes 3145732
  2.5 232.6 %collective-permute-start.3 = (f32[4,1,8192]{2,1,0:T(1,128)}, f32[4,1,8192]{2,1,0:T(1,128)}, u32[]{:S(2)}, u32[]{:S(2)}) collective-permute-start(f32[4,1,8192]{2,1,0:T(1,128)} %get-tuple-element.431), channel_id=1, source_target_pairs={{1,0},{2,1},{3,2},{4,3},{5,4},{6,5},{7,6},{9,8},{10,9},{11,10},{12... | collective-permute-start | bytes 393224 | tf_op jit(solution)/shard_map/ppermute | solution.py:24
  3.9 231.2 %collective-permute-start.4 = (f32[4,1,8192]{2,1,0:T(1,128)}, f32[4,1,8192]{2,1,0:T(1,128)}, u32[]{:S(2)}, u32[]{:S(2)}) collective-permute-start(f32[4,1,8192]{2,1,0:T(1,128)} %get-tuple-element.432), channel_id=1, source_target_pairs={{0,1},{1,2},{2,3},{3,4},{4,5},{5,6},{6,7},{8,9},{9,10},{10,11},{11... | collective-permute-start | bytes 393224 | tf_op jit(solution)/shard_map/ppermute | solution.py:22
  13.5 15.5 %copy-start.9 = (s32[8,8192]{1,0:T(8,128)S(1)}, s32[8,8192]{1,0:T(8,128)}, u32[]{:S(2)}) copy-start(s32[8,8192]{1,0:T(8,128)} %param.6) | copy-start | bytes 786436
  13.5 15.6 %copy-start.10 = (f32[3,4]{1,0:T(4,128)S(1)}, f32[3,4]{1,0:T(4,128)}, u32[]{:S(2)}) copy-start(f32[3,4]{1,0:T(4,128)} %param.7) | copy-start | bytes 148
  29.1 68.3 %copy-start.8 = (f32[8,8192]{1,0:T(8,128)}, f32[8,8192]{1,0:T(8,128)S(1)}, u32[]{:S(2)}) copy-start(f32[8,8192]{1,0:T(8,128)S(1)} %get-tuple-element.440) | copy-start | bytes 786436
  29.1 102.3 %copy-start.7 = (f32[8,8192]{1,0:T(8,128)}, f32[8,8192]{1,0:T(8,128)S(1)}, u32[]{:S(2)}) copy-start(f32[8,8192]{1,0:T(8,128)S(1)} %get-tuple-element.439) | copy-start | bytes 786436
  209.5 20.0 %copy-start.2 = (f32[4,4,4,2048]{3,2,1,0:T(4,128)}, f32[4,4,4,2048]{3,2,1,0:T(4,128)S(1)}, u32[]{:S(2)}) copy-start(f32[4,4,4,2048]{3,2,1,0:T(4,128)S(1)} %all_gather.6) | copy-start | bytes 1572868
  233.2 2.8 copy-start.1
  240.3 5.7 collective-permute-start.5
  241.6 5.9 collective-permute-start.6
  249.6 6.1 collective-permute-start.7
  250.9 6.7 collective-permute-start.8
  259.8 5.9 collective-permute-start.10
  263.7 7.0 %collective-permute-start.9 = (f32[4,1,8192]{2,1,0:T(1,128)S(1)}, f32[4,1,8192]{2,1,0:T(1,128)S(1)}, u32[]{:S(2)}, u32[]{:S(2)}) collective-permute-start(f32[4,1,8192]{2,1,0:T(1,128)S(1)} %get-tuple-element.409), channel_id=1, source_target_pairs={{1,0},{2,1},{3,2},{4,3},{5,4},{6,5},{7,6},{9,8},{10,9},{11,10},{12... | collective-permute-start | bytes 393224 | tf_op jit(solution)/shard_map/ppermute | solution.py:24
  272.2 98.7 %copy-start.5 = (f32[1,8,8192]{2,1,0:T(8,128)}, f32[1,8,8192]{2,1,0:T(8,128)S(1)}, u32[]{:S(2)}) copy-start(f32[1,8,8192]{2,1,0:T(8,128)S(1)} %get-tuple-element.394) | copy-start | bytes 786436
  429.0 3.2 copy-start.3
  429.0 3.2 copy-start.4
  467.9 3.8 collective-permute-start
  469.2 4.7 collective-permute-start.1
  474.4 9.7 %collective-permute-start.2 = (f32[4,4,2048]{2,1,0:T(4,128)S(1)}, f32[4,4,2048]{2,1,0:T(4,128)S(1)}, u32[]{:S(2)}, u32[]{:S(2)}) collective-permute-start(f32[4,4,2048]{2,1,0:T(4,128)S(1)} %get-tuple-element.570), channel_id=1, source_target_pairs={{0,8},{8,16},{16,24},{1,9},{9,17},{17,25},{2,10},{10,18},{18,26},{... | collective-permute-start | bytes 393224 | tf_op jit(solution)/shard_map/while/body/eval_jaxpr/ppermute | solution.py:34
  518.8 4.5 collective-permute-start
  520.7 4.7 collective-permute-start.1
  525.9 11.4 %collective-permute-start.2 = (f32[4,4,2048]{2,1,0:T(4,128)S(1)}, f32[4,4,2048]{2,1,0:T(4,128)S(1)}, u32[]{:S(2)}, u32[]{:S(2)}) collective-permute-start(f32[4,4,2048]{2,1,0:T(4,128)S(1)} %get-tuple-element.570), channel_id=1, source_target_pairs={{0,8},{8,16},{16,24},{1,9},{9,17},{17,25},{2,10},{10,18},{18,26},{... | collective-permute-start | bytes 393224 | tf_op jit(solution)/shard_map/while/body/eval_jaxpr/ppermute | solution.py:34
  571.0 5.3 collective-permute-start
  573.7 4.7 collective-permute-start.1
  578.9 11.5 %collective-permute-start.2 = (f32[4,4,2048]{2,1,0:T(4,128)S(1)}, f32[4,4,2048]{2,1,0:T(4,128)S(1)}, u32[]{:S(2)}, u32[]{:S(2)}) collective-permute-start(f32[4,4,2048]{2,1,0:T(4,128)S(1)} %get-tuple-element.570), channel_id=1, source_target_pairs={{0,8},{8,16},{16,24},{1,9},{9,17},{17,25},{2,10},{10,18},{18,26},{... | collective-permute-start | bytes 393224 | tf_op jit(solution)/shard_map/while/body/eval_jaxpr/ppermute | solution.py:34
  624.1 5.3 collective-permute-start
  626.8 4.7 collective-permute-start.1
  632.1 11.5 %collective-permute-start.2 = (f32[4,4,2048]{2,1,0:T(4,128)S(1)}, f32[4,4,2048]{2,1,0:T(4,128)S(1)}, u32[]{:S(2)}, u32[]{:S(2)}) collective-permute-start(f32[4,4,2048]{2,1,0:T(4,128)S(1)} %get-tuple-element.570), channel_id=1, source_target_pairs={{0,8},{8,16},{16,24},{1,9},{9,17},{17,25},{2,10},{10,18},{18,26},{... | collective-permute-start | bytes 393224 | tf_op jit(solution)/shard_map/while/body/eval_jaxpr/ppermute | solution.py:34
  659.7 18.2 %copy-start.6 = (f32[1,8,8192]{2,1,0:T(8,128)S(1)}, f32[1,8,8192]{2,1,0:T(8,128)}, u32[]{:S(2)}) copy-start(f32[1,8,8192]{2,1,0:T(8,128)} %copy-done.5) | copy-start | bytes 786436
where the time goes:
time: 690 us; the launch traced here: 679 us
  local copies, waits for them, and re-layouts  348 us (50%)
  blocking collectives  98.9 us (14%)
  starting transfers between devices  73.2 us (11%)
  loops' own time  57.8 us (8%)
  other arithmetic  54.4 us (8%)
  waiting for transfers between devices  25.4 us (4%)
  matrix products  19.7 us (3%)
    mul x8, local copies, waits for them, and re-layouts, lookup(): fields = fields + table[:, tissue][:, None, None] * chosen[None]  136 us
    concatenate x4, local copies, waits for them, and re-layouts, biot_update(): return jnp.concatenate([shifted_disp, pressure[None]], 0)  132 us
    psum x4, blocking collectives, solve_weights(): inner_products = lax.psum(partial_value, 'space')  60 us
    another operation x1, loops' own time, shards(): final_carry = lax.fori_loop(0, slices, turn, (zero_field, zero_field))  57.8 us
    ppermute x4, starting transfers between devices, shifted(): return lax.ppermute(array, axis, pairs)  36.3 us
    ppermute x8, starting transfers between devices, extended(): lax.ppermute(tail, axis, [(i, (i + 1) % count) for i in range(ends)])  26.2 us
    reduce_sum x3, other arithmetic, restrict(): blocks.sum(axis=(2, 4, 6)).reshape(components, z_depth // 2, -1) * 0.125  25.9 us
    unnamed x24, local copies, waits for them, and re-layouts  18.7 us
  transfers between devices with their start and end apart: 20, of which 14 were waited for; matrix products, arithmetic and copies ran while one was open for 30% of the time, Pallas kernels for 0%

commit v1 on v0

v1 whole, which is shorter than its diff:
```python
import functools
import jax
import jax.numpy as jnp
from jax import lax
from jax.experimental import pallas as pl
from jax.experimental.pallas import tpu as pltpu
from jax.sharding import PartitionSpec as P

NX = 32
FINE = 4
CHUNKS = 4
BLOCK = 4

fine_tau = 0.1
coarse_tau = 0.4
MESH = pl.DeviceIdType.MESH


def kernel(
    slices, spaces, starts_ref, labels_ref, table_ref, out_ref,
    field_a, field_b, coefs, halo, pair_lo, pair_hi, coarse_coefs,
    all_ru, all_rf, gram_buf, dot_buf, padded, expanded, layer_out, layer_in, defect_ref, corr_ref,
    halo_send, halo_recv, ru_send, ru_recv, rf_send, rf_recv,
    gram_send, gram_recv, dot_send, dot_recv, layer_send, layer_recv,
):
    tm = lax.axis_index("tm")
    me = lax.axis_index("space")
    length = starts_ref.shape[-1] // NX
    depth = starts_ref.shape[2]
    half = NX // 2
    rows = half * depth // 2
    f32 = jnp.float32

    barrier = pltpu.get_barrier_semaphore()
    for off in range(1, slices):
        pl.semaphore_signal(
            barrier, inc=1, device_id={"tm": lax.rem(tm + off, slices)}, device_id_type=MESH
        )
    for off in range(1, spaces):
        pl.semaphore_signal(
            barrier, inc=1, device_id={"space": lax.rem(me + off, spaces)}, device_id_type=MESH
        )

    has_down = me > 0
    has_up = me < spaces - 1

    zero_plane = jnp.zeros((4, 1, depth, length), f32)
    for buf in (field_a, field_b):
        buf[:, pl.ds(0, 1)] = zero_plane
        buf[:, pl.ds(NX + 1, 1)] = zero_plane

    def load(x, carry):
        cols = pl.ds(pl.multiple_of(x * length, length), length)
        field_a[:, x + 1] = starts_ref[0, :, :, cols]
        return carry

    lax.fori_loop(0, NX, load, 0, unroll=4)

    pl.semaphore_wait(barrier, slices - 1 + spaces - 1)

    span = NX // CHUNKS

    def halo_copies(step, chunk, buf):
        xs = pl.ds(1 + chunk * span, span)
        to = pl.ds(chunk * span, span)
        up = pltpu.make_async_remote_copy(
            src_ref=buf.at[:, xs, pl.ds(depth - 1, 1), :],
            dst_ref=halo.at[step, 0, :, to],
            send_sem=halo_send.at[step, 0, chunk],
            recv_sem=halo_recv.at[step, 0, chunk],
            device_id={"space": lax.rem(me + 1, spaces)},
            device_id_type=MESH,
        )
        down = pltpu.make_async_remote_copy(
            src_ref=buf.at[:, xs, pl.ds(0, 1), :],
            dst_ref=halo.at[step, 1, :, to],
            send_sem=halo_send.at[step, 1, chunk],
            recv_sem=halo_recv.at[step, 1, chunk],
            device_id={"space": lax.rem(me + spaces - 1, spaces)},
            device_id_type=MESH,
        )
        return up, down

    def start_pair(pair):
        @pl.when(has_up)
        def _():
            pair[0].start()

        @pl.when(has_down)
        def _():
            pair[1].start()

    def wait_pair(pair):
        @pl.when(has_up)
        def _():
            pair[0].wait_send()
            pair[1].wait_recv()

        @pl.when(has_down)
        def _():
            pair[1].wait_send()
            pair[0].wait_recv()

    for chunk in range(CHUNKS):
        start_pair(halo_copies(0, chunk, field_a))

    @pl.when(jnp.logical_not(has_down))
    def _():
        for step in range(FINE):
            halo[step, 0] = jnp.zeros(halo.shape[2:], f32)
        for turn in range(slices - 1):
            layer_in[turn, 0] = jnp.zeros(layer_in.shape[2:], f32)

    @pl.when(jnp.logical_not(has_up))
    def _():
        for step in range(FINE):
            halo[step, 1] = jnp.zeros(halo.shape[2:], f32)
        for turn in range(slices - 1):
            layer_in[turn, 1] = jnp.zeros(layer_in.shape[2:], f32)

    scales = (fine_tau, fine_tau, fine_tau * 0.5)

    def fill(x, carry):
        cols = pl.ds(pl.multiple_of(x * length, length), length)
        labels = labels_ref[:, cols]
        for k in range(3):
            value = jnp.zeros(labels.shape, f32)
            for tissue in range(table_ref.shape[1]):
                value = jnp.where(labels == tissue, table_ref[k, tissue] * scales[k], value)
            coefs[k, x] = value
        return carry

    lax.fori_loop(0, NX, fill, 0, unroll=2)

    lane = lax.broadcasted_iota(jnp.int32, (length // 2, length // 2), 0)
    place = lax.broadcasted_iota(jnp.int32, (length // 2, length // 2), 1)
    quarter = length // 4
    pick_lo = jnp.where(lane // 2 == place, 0.125, 0.0).astype(f32)
    pick_hi = jnp.where(lane // 2 + quarter == place, 0.125, 0.0).astype(f32)

    def restrict(buf, first, count):
        def pair_up(i, carry):
            for c in range(count):
                both = buf[c, first + 2 * i] + buf[c, first + 2 * i + 1]
                at = pl.ds(pl.multiple_of((c * half + i) * depth, depth), depth)
                pair_lo[at, :] = both[:, : length // 2]
                pair_hi[at, :] = both[:, length // 2 :]
            return carry

        lax.fori_loop(0, half, pair_up, 0, unroll=4)
        even = pl.ds(0, count * rows, stride=2)
        odd = pl.ds(1, count * rows, stride=2)
        low = pair_lo[even, :] + pair_lo[odd, :]
        high = pair_hi[even, :] + pair_hi[odd, :]
        dot = functools.partial(
            jnp.dot, precision=lax.Precision.HIGHEST, preferred_element_type=f32
        )
        return dot(low, pick_lo) + dot(high, pick_hi)

    def gather_copies(buf, sends, recvs):
        return [
            pltpu.make_async_remote_copy(
                src_ref=buf.at[tm], dst_ref=buf.at[tm],
                send_sem=sends.at[off - 1], recv_sem=recvs.at[off - 1],
                device_id={"tm": lax.rem(tm + off, slices)}, device_id_type=MESH,
            )
            for off in range(1, slices)
        ]

    def space_copies(part, sends, recvs):
        return [
            pltpu.make_async_remote_copy(
                src_ref=part, dst_ref=part,
                send_sem=sends.at[off - 1], recv_sem=recvs.at[off - 1],
                device_id={"space": lax.rem(me + off, spaces)}, device_id_type=MESH,
            )
            for off in range(1, spaces)
        ]

    all_ru[tm] = restrict(field_a, 1, 4)
    ru_copies = gather_copies(all_ru, ru_send, ru_recv)
    for copy in ru_copies:
        copy.start()

    coarse_coefs[...] = restrict(coefs, 0, 3)

    row = lax.broadcasted_iota(jnp.int32, (1, depth, length), 1)
    col = lax.broadcasted_iota(jnp.int32, (1, depth, length), 2)
    gram_copies = None
    bufs = (field_a, field_b)
    for step in range(FINE):
        src, dst = bufs[step % 2], bufs[(step + 1) % 2]
        for chunk in range(CHUNKS):
            wait_pair(halo_copies(step, chunk, src))

            def block(b, carry):
                x0 = chunk * span + b * BLOCK
                now, dx, dy, dz, lap = [], [], [], [], []
                for c in range(4):
                    v = src[c, pl.ds(x0 + 1, BLOCK)]
                    x_up = src[c, pl.ds(x0 + 2, BLOCK)]
                    x_dn = src[c, pl.ds(x0, BLOCK)]
                    y_up = jnp.where(col == length - 1, 0.0, pltpu.roll(v, length - 1, 2))
                    y_dn = jnp.where(col == 0, 0.0, pltpu.roll(v, 1, 2))
                    z_up = jnp.where(
                        row == depth - 1, halo[step, 1, c, pl.ds(x0, BLOCK)], pltpu.roll(v, depth - 1, 1)
                    )
                    z_dn = jnp.where(row == 0, halo[step, 0, c, pl.ds(x0, BLOCK)], pltpu.roll(v, 1, 1))
                    now.append(v)
                    lap.append(x_up + x_dn + y_up + y_dn + z_up + z_dn - 6.0 * v)
                    if c in (0, 3):
                        dx.append(x_up - x_dn)
                    if c in (1, 3):
                        dy.append(y_up - y_dn)
                    if c in (2, 3):
                        dz.append(z_up - z_dn)
                shear = coefs[0, pl.ds(x0, BLOCK)]
                perm = coefs[1, pl.ds(x0, BLOCK)]
                couple = coefs[2, pl.ds(x0, BLOCK)]
                grads = (dx[1], dy[1], dz[1])
                for c in range(3):
                    dst[c, pl.ds(x0 + 1, BLOCK)] = now[c] + (shear * lap[c] - couple * grads[c])
                dst[3, pl.ds(x0 + 1, BLOCK)] = now[3] + (
                    perm * lap[3] - couple * (dx[0] + dy[0] + dz[0])
                )
                return carry

            lax.fori_loop(0, span // BLOCK, block, 0)
            if step + 1 < FINE:
                start_pair(halo_copies(step + 1, chunk, dst))
        if step == FINE - 2:
            for copy in ru_copies:
                copy.wait()
            line = 0
            for a in range(slices):
                for b in range(a + 1):
                    gram_buf[me, pl.ds(line, 1), :] = jnp.sum(
                        all_ru[a] * all_ru[b], axis=0, keepdims=True
                    )
                    line += 1
            for spare in range(line, gram_buf.shape[1]):
                gram_buf[me, pl.ds(spare, 1), :] = jnp.zeros((1, length // 2), f32)
            gram_copies = space_copies(gram_buf.at[me], gram_send, gram_recv)
            for copy in gram_copies:
                copy.start()
    final = bufs[FINE % 2]

    all_rf[tm] = restrict(final, 1, 4)
    rf_copies = gather_copies(all_rf, rf_send, rf_recv)
    for copy in rf_copies:
        copy.start()

    def total(buf):
        summed = buf[0]
        for s in range(1, spaces):
            summed = summed + buf[s]
        return jnp.broadcast_to(jnp.sum(summed, axis=1, keepdims=True), summed.shape)

    for copy in gram_copies:
        copy.wait()
    gram = total(gram_buf)
    entry = {}
    line = 0
    for a in range(slices):
        for b in range(a + 1):
            entry[a, b] = gram[line : line + 1]
            line += 1
    factor, inverse = {}, {}
    for b in range(slices):
        diag = entry[b, b]
        for k in range(b):
            diag = diag - factor[b, k] * factor[b, k]
        factor[b, b] = jnp.sqrt(diag)
        inverse[b] = 1.0 / factor[b, b]
        for a in range(b + 1, slices):
            value = entry[a, b]
            for k in range(b):
                value = value - factor[a, k] * factor[b, k]
            factor[a, b] = value * inverse[b]

    padded[...] = jnp.zeros(padded.shape, f32)
    corr_ref[...] = jnp.zeros(corr_ref.shape, f32)
    for copy in rf_copies:
        copy.wait()

    crow = lax.broadcasted_iota(jnp.int32, (rows, length // 2), 0)
    ccol = lax.broadcasted_iota(jnp.int32, (rows, length // 2), 1)
    per = depth // 2
    at_top = lax.rem(crow, per) == per - 1
    at_bottom = lax.rem(crow, per) == 0
    layers = 4 * half

    def coarse_part(k):
        return coarse_coefs[pl.ds(k * rows, rows), :]

    lap_scale = coarse_tau / 4.0 / fine_tau
    div_scale = coarse_tau / 4.0 / (fine_tau * 0.5)

    defect_ref[...] = all_rf[0] - all_ru[1]
    for j in range(1, slices):
        turn = j - 1
        defect = defect_ref[...]
        for a in range(slices):
            dot_buf[turn, me, pl.ds(a, 1), :] = jnp.sum(all_ru[a] * defect, axis=0, keepdims=True)
        for spare in range(slices, dot_buf.shape[2]):
            dot_buf[turn, me, pl.ds(spare, 1), :] = jnp.zeros((1, length // 2), f32)
        copies = space_copies(dot_buf.at[turn, me], dot_send.at[turn], dot_recv.at[turn])
        for copy in copies:
            copy.start()
        for copy in copies:
            copy.wait()
        inner = total(dot_buf.at[turn])
        forward, weights = [], [None] * slices
        for a in range(slices):
            value = inner[a : a + 1]
            for k in range(a):
                value = value - factor[a, k] * forward[k]
            forward.append(value * inverse[a])
        for a in reversed(range(slices)):
            value = forward[a]
            for k in range(a + 1, slices):
                value = value - factor[k, a] * weights[k]
            weights[a] = value * inverse[a]

        rest = defect
        for a in range(slices):
            rest = rest - weights[a] * all_ru[a]
        defect_ref[...] = rest
        layer_out[turn, 0] = defect_ref[pl.ds(per - 1, layers, stride=per), :]
        layer_out[turn, 1] = defect_ref[pl.ds(0, layers, stride=per), :]
        pair = [
            pltpu.make_async_remote_copy(
                src_ref=layer_out.at[turn, way], dst_ref=layer_in.at[turn, way],
                send_sem=layer_send.at[turn, way], recv_sem=layer_recv.at[turn, way],
                device_id={"space": lax.rem(me + by, spaces)}, device_id_type=MESH,
            )
            for way, by in ((0, 1), (1, spaces - 1))
        ]
        start_pair(pair)
        for c in range(4):
            padded[c, pl.ds(8, rows), :] = rest[c * rows : (c + 1) * rows]
        blend = weights[0] * all_rf[0]
        for a in range(1, slices):
            blend = blend + weights[a] * all_rf[a]
        wait_pair(pair)
        expanded[0, pl.ds(0, layers, stride=per), :] = layer_in[turn, 0]
        expanded[1, pl.ds(per - 1, layers, stride=per), :] = layer_in[turn, 1]
        now, dx, dy, dz, lap = [], [], [], [], []
        width = length // 2
        for c in range(4):
            v = padded[c, pl.ds(8, rows), :]
            x_up = padded[c, pl.ds(8 + per, rows), :]
            x_dn = padded[c, pl.ds(8 - per, rows), :]
            y_up = jnp.where(ccol == width - 1, 0.0, pltpu.roll(v, width - 1, 1))
            y_dn = jnp.where(ccol == 0, 0.0, pltpu.roll(v, 1, 1))
            z_up = jnp.where(at_top, expanded[1, pl.ds(c * rows, rows), :], padded[c, pl.ds(9, rows), :])
            z_dn = jnp.where(at_bottom, expanded[0, pl.ds(c * rows, rows), :], padded[c, pl.ds(7, rows), :])
            now.append(v)
            lap.append((x_up + x_dn + y_up + y_dn + z_up + z_dn - 6.0 * v) * lap_scale)
            if c in (0, 3):
                dx.append(x_up - x_dn)
            if c in (1, 3):
                dy.append(y_up - y_dn)
            if c in (2, 3):
                dz.append(z_up - z_dn)
        couple = coarse_part(2) * div_scale
        grads = (dx[1], dy[1], dz[1])
        parts = [now[c] + (coarse_part(0) * lap[c] - couple * grads[c]) for c in range(3)]
        parts.append(now[3] + (coarse_part(1) * lap[3] - couple * (dx[0] + dy[0] + dz[0])))
        corr = jnp.concatenate(parts, axis=0) + blend

        @pl.when(tm == j)
        def _():
            corr_ref[...] = corr

        if j + 1 < slices:
            defect_ref[...] = all_rf[j] + corr - all_ru[j + 1]

    spread_lo = jnp.where(lane == place // 2, 1.0, 0.0).astype(f32)
    spread_hi = jnp.where(lane == place // 2 + quarter, 1.0, 0.0).astype(f32)
    own = corr_ref[...]
    for buf, spread in ((pair_lo, spread_lo), (pair_hi, spread_hi)):
        wide = jnp.dot(own, spread, precision=lax.Precision.HIGHEST, preferred_element_type=f32)
        buf[pl.ds(0, 4 * rows, stride=2), :] = wide
        buf[pl.ds(1, 4 * rows, stride=2), :] = wide

    def finish(i, carry):
        for c in range(4):
            at = pl.ds(pl.multiple_of((c * half + i) * depth, depth), depth)
            add = jnp.concatenate([pair_lo[at, :], pair_hi[at, :]], axis=1)
            for k in range(2):
                cols = pl.ds(pl.multiple_of((2 * i + k) * length, length), length)
                out_ref[0, c, :, cols] = final[c, 2 * i + k + 1] + add
        return carry

    lax.fori_loop(0, half, finish, 0, unroll=2)


def shards(slices, spaces, starts, labels, coef_table):
    f32 = jnp.float32
    depth, plane = starts.shape[2:]
    length = plane // NX
    width = length // 2
    half = NX // 2
    rows = half * depth // 2
    gram_rows = -(-(slices * (slices + 1) // 2) // 8) * 8
    dot_rows = -(-slices // 8) * 8
    vmem = pl.BlockSpec(memory_space=pltpu.VMEM)
    dma = pltpu.SemaphoreType.DMA
    return pl.pallas_call(
        functools.partial(kernel, slices, spaces),
        out_shape=jax.ShapeDtypeStruct(starts.shape, f32),
        in_specs=[vmem, vmem, pl.BlockSpec(memory_space=pltpu.SMEM)],
        out_specs=vmem,
        scratch_shapes=[
            pltpu.VMEM((4, NX + 2, depth, length), f32),
            pltpu.VMEM((4, NX + 2, depth, length), f32),
            pltpu.VMEM((3, NX, depth, length), f32),
            pltpu.VMEM((FINE, 2, 4, NX, 1, length), f32),
            pltpu.VMEM((8 * rows, width), f32),
            pltpu.VMEM((8 * rows, width), f32),
            pltpu.VMEM((3 * rows, width), f32),
            pltpu.VMEM((slices, 4 * rows, width), f32),
            pltpu.VMEM((slices, 4 * rows, width), f32),
            pltpu.VMEM((spaces, gram_rows, width), f32),
            pltpu.VMEM((slices - 1, spaces, dot_rows, width), f32),
            pltpu.VMEM((4, rows + 16, width), f32),
            pltpu.VMEM((2, 4 * rows, width), f32),
            pltpu.VMEM((slices - 1, 2, 4 * half, width), f32),
            pltpu.VMEM((slices - 1, 2, 4 * half, width), f32),
            pltpu.VMEM((4 * rows, width), f32),
            pltpu.VMEM((4 * rows, width), f32),
            dma((FINE, 2, CHUNKS)),
            dma((FINE, 2, CHUNKS)),
            dma((slices - 1,)),
            dma((slices - 1,)),
            dma((slices - 1,)),
            dma((slices - 1,)),
            dma((spaces - 1,)),
            dma((spaces - 1,)),
            dma((slices - 1, spaces - 1)),
            dma((slices - 1, spaces - 1)),
            dma((slices - 1, 2)),
            dma((slices - 1, 2)),
        ],
        compiler_params=pltpu.CompilerParams(
            collective_id=0, has_side_effects=True, vmem_limit_bytes=48 * 1024 * 1024
        ),
    )(starts, labels, coef_table)


def solution(mesh):
    placed = (P("tm", None, "space", None), P("space", None), P())
    return jax.shard_map(
        functools.partial(shards, mesh.shape["tm"], mesh.shape["space"]),
        mesh=mesh, in_specs=placed, out_specs=P("tm", None, "space", None), check_vma=False,
    )
```

time: 690 us -> 66.4 us (0.10)
  the two profiles are of different devices: /device:TPU:1 before, /device:TPU:0 now
where the time goes in v1:
time: 66.4 us; the launch traced here: 66.2 us
  Pallas kernels  62.4 us (94%)
  local copies, waits for them, and re-layouts  3.83 us (6%)
    pallas_call x1, Pallas kernels, shards(): pl.pallas_call(functools.partial(kernel, slices, spaces), out_shape=jax.S...  62.4 us
    unnamed x7, local copies, waits for them, and re-layouts  3.83 us

profile of v1, /device:TPU:0, one launch (start us, length us, event | category | flops | bytes accessed | tf_op | source)
XLA Modules:
  0.0 66.2 jit_solution(4887314205640853761)
XLA Ops:
  0.0 0.0 copy-start
  0.0 1.2 %copy-done = f32[1,4,8,8192]{3,2,1,0:T(8,128)S(1)} copy-done((f32[1,4,8,8192]{3,2,1,0:T(8,128)S(1)}, f32[1,4,8,8192]{3,2,1,0:T(8,128)}, u32[]{:S(2)}) %copy-start) | copy-done | bytes 1048600
  1.2 0.0 copy-start.1
  1.2 0.9 %copy-done.1 = s32[8,8192]{1,0:T(8,128)S(1)} copy-done((s32[8,8192]{1,0:T(8,128)S(1)}, s32[8,8192]{1,0:T(8,128)}, u32[]{:S(2)}) %copy-start.1) | copy-done | bytes 262168
  2.2 0.0 copy-start.2
  2.2 0.7 %copy-done.2 = f32[3,4]{1,0:T(4,128)S(1)} copy-done((f32[3,4]{1,0:T(4,128)S(1)}, f32[3,4]{1,0:T(4,128)}, u32[]{:S(2)}) %copy-start.2) | copy-done | bytes 72
  2.9 62.4 %shard_map.37 = f32[1,4,8,8192]{3,2,1,0:T(8,128)S(1)} custom-call(f32[1,4,8,8192]{3,2,1,0:T(8,128)S(1)} %copy-done, s32[8,8192]{1,0:T(8,128)S(1)} %copy-done.1, f32[3,4]{1,0:T(4,128)S(1)} %copy-done.2), custom_call_target="tpu_custom_call" | custom-call | tf_op jit(solution)/shard_map/pallas_call | solution.py:410
  65.2 1.0 %copy.5 = f32[1,4,8,8192]{3,2,1,0:T(8,128)} copy(f32[1,4,8,8192]{3,2,1,0:T(8,128)S(1)} %shard_map.37) | data formatting | bytes 2097152
Async XLA Ops:
  0.0 1.2 %copy-start = (f32[1,4,8,8192]{3,2,1,0:T(8,128)S(1)}, f32[1,4,8,8192]{3,2,1,0:T(8,128)}, u32[]{:S(2)}) copy-start(f32[1,4,8,8192]{3,2,1,0:T(8,128)} %starts_ref.1) | copy-start | bytes 3145732
  1.2 0.9 %copy-start.1 = (s32[8,8192]{1,0:T(8,128)S(1)}, s32[8,8192]{1,0:T(8,128)}, u32[]{:S(2)}) copy-start(s32[8,8192]{1,0:T(8,128)} %labels_ref.1) | copy-start | bytes 786436
  2.2 0.7 %copy-start.2 = (f32[3,4]{1,0:T(4,128)S(1)}, f32[3,4]{1,0:T(4,128)}, u32[]{:S(2)}) copy-start(f32[3,4]{1,0:T(4,128)} %table_ref.1) | copy-start | bytes 148

commit v2 on v1

--- a/solution.py
+++ b/solution.py
@@ -17,11 +17,13 @@
 
 
 def kernel(
-    slices, spaces, starts_ref, labels_ref, table_ref, out_ref,
+    slices, spaces, starts_hbm, labels_hbm, table_ref, out_ref,
+    starts_ref, labels_ref,
     field_a, field_b, coefs, halo, pair_lo, pair_hi, coarse_coefs,
     all_ru, all_rf, gram_buf, dot_buf, padded, expanded, layer_out, layer_in, defect_ref, corr_ref,
     halo_send, halo_recv, ru_send, ru_recv, rf_send, rf_recv,
     gram_send, gram_recv, dot_send, dot_recv, layer_send, layer_recv,
+    edges_out, all_edges, images, fetch_sem, edge_send, edge_recv, edges_send, edges_recv,
 ):
     tm = lax.axis_index("tm")
     me = lax.axis_index("space")
@@ -31,6 +33,12 @@
     rows = half * depth // 2
     f32 = jnp.float32
 
+    fetch = (
+        pltpu.make_async_copy(starts_hbm, starts_ref, fetch_sem.at[0]),
+        pltpu.make_async_copy(labels_hbm, labels_ref, fetch_sem.at[1]),
+    )
+    for copy in fetch:
+        copy.start()
     barrier = pltpu.get_barrier_semaphore()
     for off in range(1, slices):
         pl.semaphore_signal(
@@ -49,14 +57,14 @@
         buf[:, pl.ds(0, 1)] = zero_plane
         buf[:, pl.ds(NX + 1, 1)] = zero_plane
 
+    fetch[0].wait()
+
     def load(x, carry):
         cols = pl.ds(pl.multiple_of(x * length, length), length)
         field_a[:, x + 1] = starts_ref[0, :, :, cols]
         return carry
 
     lax.fori_loop(0, NX, load, 0, unroll=4)
-
-    pl.semaphore_wait(barrier, slices - 1 + spaces - 1)
 
     span = NX // CHUNKS
 
@@ -101,15 +109,13 @@
             pair[1].wait_send()
             pair[0].wait_recv()
 
-    for chunk in range(CHUNKS):
-        start_pair(halo_copies(0, chunk, field_a))
-
     @pl.when(jnp.logical_not(has_down))
     def _():
         for step in range(FINE):
             halo[step, 0] = jnp.zeros(halo.shape[2:], f32)
         for turn in range(slices - 1):
             layer_in[turn, 0] = jnp.zeros(layer_in.shape[2:], f32)
+        all_edges[tm, 0] = jnp.zeros(all_edges.shape[2:], f32)
 
     @pl.when(jnp.logical_not(has_up))
     def _():
@@ -117,7 +123,9 @@
             halo[step, 1] = jnp.zeros(halo.shape[2:], f32)
         for turn in range(slices - 1):
             layer_in[turn, 1] = jnp.zeros(layer_in.shape[2:], f32)
-
+        all_edges[tm, 1] = jnp.zeros(all_edges.shape[2:], f32)
+
+    fetch[1].wait()
     scales = (fine_tau, fine_tau, fine_tau * 0.5)
 
     def fill(x, carry):
@@ -177,12 +185,71 @@
             for off in range(1, spaces)
         ]
 
-    all_ru[tm] = restrict(field_a, 1, 4)
+    per = depth // 2
+    layers = 4 * half
+    own_start = restrict(field_a, 1, 4)
+    all_ru[tm] = own_start
+    defect_ref[...] = own_start
+    edges_out[0] = defect_ref[pl.ds(per - 1, layers, stride=per), :]
+    edges_out[1] = defect_ref[pl.ds(0, layers, stride=per), :]
+    coarse_coefs[...] = restrict(coefs, 0, 3)
+    padded[...] = jnp.zeros(padded.shape, f32)
+    corr_ref[...] = jnp.zeros(corr_ref.shape, f32)
+
+    pl.semaphore_wait(barrier, slices - 1 + spaces - 1)
+    for chunk in range(CHUNKS):
+        start_pair(halo_copies(0, chunk, field_a))
+    edge_pair = [
+        pltpu.make_async_remote_copy(
+            src_ref=edges_out.at[way], dst_ref=all_edges.at[tm, way],
+            send_sem=edge_send.at[way], recv_sem=edge_recv.at[way],
+            device_id={"space": lax.rem(me + by, spaces)}, device_id_type=MESH,
+        )
+        for way, by in ((0, 1), (1, spaces - 1))
+    ]
+    start_pair(edge_pair)
     ru_copies = gather_copies(all_ru, ru_send, ru_recv)
     for copy in ru_copies:
         copy.start()
 
-    coarse_coefs[...] = restrict(coefs, 0, 3)
+    crow = lax.broadcasted_iota(jnp.int32, (rows, length // 2), 0)
+    ccol = lax.broadcasted_iota(jnp.int32, (rows, length // 2), 1)
+    at_top = lax.rem(crow, per) == per - 1
+    at_bottom = lax.rem(crow, per) == 0
+    lap_scale = coarse_tau / 4.0 / fine_tau
+    div_scale = coarse_tau / 4.0 / (fine_tau * 0.5)
+
+    def coarse_part(k):
+        return coarse_coefs[pl.ds(k * rows, rows), :]
+
+    def coarse_image(edges):
+        expanded[0, pl.ds(0, layers, stride=per), :] = edges[0]
+        expanded[1, pl.ds(per - 1, layers, stride=per), :] = edges[1]
+        now, dx, dy, dz, lap = [], [], [], [], []
+        width = length // 2
+        for c in range(4):
+            v = padded[c, pl.ds(8, rows), :]
+            x_up = padded[c, pl.ds(8 + per, rows), :]
+            x_dn = padded[c, pl.ds(8 - per, rows), :]
+            y_up = jnp.where(ccol == width - 1, 0.0, pltpu.roll(v, width - 1, 1))
+            y_dn = jnp.where(ccol == 0, 0.0, pltpu.roll(v, 1, 1))
+            z_up = jnp.where(at_top, expanded[1, pl.ds(c * rows, rows), :], padded[c, pl.ds(9, rows), :])
+            z_dn = jnp.where(at_bottom, expanded[0, pl.ds(c * rows, rows), :], padded[c, pl.ds(7, rows), :])
+            now.append(v)
+            lap.append((x_up + x_dn + y_up + y_dn + z_up + z_dn - 6.0 * v) * lap_scale)
+            if c in (0, 3):
+                dx.append(x_up - x_dn)
+            if c in (1, 3):
+                dy.append(y_up - y_dn)
+            if c in (2, 3):
+                dz.append(z_up - z_dn)
+        couple = coarse_part(2) * div_scale
+        grads = (dx[1], dy[1], dz[1])
+        parts = [now[c] + (coarse_part(0) * lap[c] - couple * grads[c]) for c in range(3)]
+        parts.append(now[3] + (coarse_part(1) * lap[3] - couple * (dx[0] + dy[0] + dz[0])))
+        return jnp.concatenate(parts, axis=0)
+
+    edges_copies = gather_copies(all_edges, edges_send, edges_recv)
 
     row = lax.broadcasted_iota(jnp.int32, (1, depth, length), 1)
     col = lax.broadcasted_iota(jnp.int32, (1, depth, length), 2)
@@ -228,6 +295,10 @@
             lax.fori_loop(0, span // BLOCK, block, 0)
             if step + 1 < FINE:
                 start_pair(halo_copies(step + 1, chunk, dst))
+        if step == 0:
+            wait_pair(edge_pair)
+            for copy in edges_copies:
+                copy.start()
         if step == FINE - 2:
             for copy in ru_copies:
                 copy.wait()
@@ -243,11 +314,33 @@
             gram_copies = space_copies(gram_buf.at[me], gram_send, gram_recv)
             for copy in gram_copies:
                 copy.start()
+            for copy in edges_copies:
+                copy.wait()
+
+            def image_of(a, carry):
+                for c in range(4):
+                    padded[c, pl.ds(8, rows), :] = all_ru[a, pl.ds(c * rows, rows), :]
+                images[a] = coarse_image(all_edges.at[a])
+                return carry
+
+            lax.fori_loop(0, slices, image_of, 0)
     final = bufs[FINE % 2]
 
     all_rf[tm] = restrict(final, 1, 4)
-    rf_copies = gather_copies(all_rf, rf_send, rf_recv)
-    for copy in rf_copies:
+    sibling = tm + 1 - 2 * lax.rem(tm, 2)
+
+    def rf_copy(slot, index, target):
+        return pltpu.make_async_remote_copy(
+            src_ref=all_rf.at[slot], dst_ref=all_rf.at[slot],
+            send_sem=rf_send.at[index], recv_sem=rf_recv.at[index],
+            device_id={"tm": target}, device_id_type=MESH,
+        )
+
+    far = [
+        rf_copy(tm, off - 1, lax.rem(tm + off, slices)) for off in range(2, slices, 2)
+    ]
+    near = [rf_copy(tm, 0, sibling)]
+    for copy in far + near:
         copy.start()
 
     def total(buf):
@@ -278,27 +371,28 @@
                 value = value - factor[a, k] * factor[b, k]
             factor[a, b] = value * inverse[b]
 
-    padded[...] = jnp.zeros(padded.shape, f32)
-    corr_ref[...] = jnp.zeros(corr_ref.shape, f32)
-    for copy in rf_copies:
+    for off, copy in zip(range(2, slices, 2), far):
         copy.wait()
-
-    crow = lax.broadcasted_iota(jnp.int32, (rows, length // 2), 0)
-    ccol = lax.broadcasted_iota(jnp.int32, (rows, length // 2), 1)
-    per = depth // 2
-    at_top = lax.rem(crow, per) == per - 1
-    at_bottom = lax.rem(crow, per) == 0
-    layers = 4 * half
-
-    def coarse_part(k):
-        return coarse_coefs[pl.ds(k * rows, rows), :]
-
-    lap_scale = coarse_tau / 4.0 / fine_tau
-    div_scale = coarse_tau / 4.0 / (fine_tau * 0.5)
+        onward = rf_copy(lax.rem(tm - off + slices, slices), off, sibling)
+        onward.start()
+        near.append(onward)
+    for copy in near:
+        copy.wait()
 
     defect_ref[...] = all_rf[0] - all_ru[1]
     for j in range(1, slices):
         turn = j - 1
+        layer_out[turn, 0] = defect_ref[pl.ds(per - 1, layers, stride=per), :]
+        layer_out[turn, 1] = defect_ref[pl.ds(0, layers, stride=per), :]
+        pair = [
+            pltpu.make_async_remote_copy(
+                src_ref=layer_out.at[turn, way], dst_ref=layer_in.at[turn, way],
+                send_sem=layer_send.at[turn, way], recv_sem=layer_recv.at[turn, way],
+                device_id={"space": lax.rem(me + by, spaces)}, device_id_type=MESH,
+            )
+            for way, by in ((0, 1), (1, spaces - 1))
+        ]
+        start_pair(pair)
         defect = defect_ref[...]
         for a in range(slices):
             dot_buf[turn, me, pl.ds(a, 1), :] = jnp.sum(all_ru[a] * defect, axis=0, keepdims=True)
@@ -307,6 +401,15 @@
         copies = space_copies(dot_buf.at[turn, me], dot_send.at[turn], dot_recv.at[turn])
         for copy in copies:
             copy.start()
+        if j == 1:
+            for a in range(slices):
+                images[a] = all_rf[a] - images[a]
+        for c in range(4):
+            padded[c, pl.ds(8, rows), :] = defect_ref[pl.ds(c * rows, rows), :]
+        wait_pair(pair)
+        image = coarse_image(layer_in.at[turn])
+        if j + 1 < slices:
+            defect_ref[...] = all_rf[j] - all_ru[j + 1]
         for copy in copies:
             copy.wait()
         inner = total(dot_buf.at[turn])
@@ -321,60 +424,16 @@
             for k in range(a + 1, slices):
                 value = value - factor[k, a] * weights[k]
             weights[a] = value * inverse[a]
-
-        rest = defect
+        corr = image
         for a in range(slices):
-            rest = rest - weights[a] * all_ru[a]
-        defect_ref[...] = rest
-        layer_out[turn, 0] = defect_ref[pl.ds(per - 1, layers, stride=per), :]
-        layer_out[turn, 1] = defect_ref[pl.ds(0, layers, stride=per), :]
-        pair = [
-            pltpu.make_async_remote_copy(
-                src_ref=layer_out.at[turn, way], dst_ref=layer_in.at[turn, way],
-                send_sem=layer_send.at[turn, way], recv_sem=layer_recv.at[turn, way],
-                device_id={"space": lax.rem(me + by, spaces)}, device_id_type=MESH,
-            )
-            for way, by in ((0, 1), (1, spaces - 1))
-        ]
-        start_pair(pair)
-        for c in range(4):
-            padded[c, pl.ds(8, rows), :] = rest[c * rows : (c + 1) * rows]
-        blend = weights[0] * all_rf[0]
-        for a in range(1, slices):
-            blend = blend + weights[a] * all_rf[a]
-        wait_pair(pair)
-        expanded[0, pl.ds(0, layers, stride=per), :] = layer_in[turn, 0]
-        expanded[1, pl.ds(per - 1, layers, stride=per), :] = layer_in[turn, 1]
-        now, dx, dy, dz, lap = [], [], [], [], []
-        width = length // 2
-        for c in range(4):
-            v = padded[c, pl.ds(8, rows), :]
-            x_up = padded[c, pl.ds(8 + per, rows), :]
-            x_dn = padded[c, pl.ds(8 - per, rows), :]
-            y_up = jnp.where(ccol == width - 1, 0.0, pltpu.roll(v, width - 1, 1))
-            y_dn = jnp.where(ccol == 0, 0.0, pltpu.roll(v, 1, 1))
-            z_up = jnp.where(at_top, expanded[1, pl.ds(c * rows, rows), :], padded[c, pl.ds(9, rows), :])
-            z_dn = jnp.where(at_bottom, expanded[0, pl.ds(c * rows, rows), :], padded[c, pl.ds(7, rows), :])
-            now.append(v)
-            lap.append((x_up + x_dn + y_up + y_dn + z_up + z_dn - 6.0 * v) * lap_scale)
-            if c in (0, 3):
-                dx.append(x_up - x_dn)
-            if c in (1, 3):
-                dy.append(y_up - y_dn)
-            if c in (2, 3):
-                dz.append(z_up - z_dn)
-        couple = coarse_part(2) * div_scale
-        grads = (dx[1], dy[1], dz[1])
-        parts = [now[c] + (coarse_part(0) * lap[c] - couple * grads[c]) for c in range(3)]
-        parts.append(now[3] + (coarse_part(1) * lap[3] - couple * (dx[0] + dy[0] + dz[0])))
-        corr = jnp.concatenate(parts, axis=0) + blend
+            corr = corr + weights[a] * images[a]
 
         @pl.when(tm == j)
         def _():
             corr_ref[...] = corr
 
         if j + 1 < slices:
-            defect_ref[...] = all_rf[j] + corr - all_ru[j + 1]
+            defect_ref[...] = defect_ref[...] + corr
 
     spread_lo = jnp.where(lane == place // 2, 1.0, 0.0).astype(f32)
     spread_hi = jnp.where(lane == place // 2 + quarter, 1.0, 0.0).astype(f32)
@@ -406,13 +465,16 @@
     gram_rows = -(-(slices * (slices + 1) // 2) // 8) * 8
     dot_rows = -(-slices // 8) * 8
     vmem = pl.BlockSpec(memory_space=pltpu.VMEM)
+    hbm = pl.BlockSpec(memory_space=pl.ANY)
     dma = pltpu.SemaphoreType.DMA
     return pl.pallas_call(
         functools.partial(kernel, slices, spaces),
         out_shape=jax.ShapeDtypeStruct(starts.shape, f32),
-        in_specs=[vmem, vmem, pl.BlockSpec(memory_space=pltpu.SMEM)],
+        in_specs=[hbm, hbm, pl.BlockSpec(memory_space=pltpu.SMEM)],
         out_specs=vmem,
         scratch_shapes=[
+            pltpu.VMEM(starts.shape, f32),
+            pltpu.VMEM(labels.shape, labels.dtype),
             pltpu.VMEM((4, NX + 2, depth, length), f32),
             pltpu.VMEM((4, NX + 2, depth, length), f32),
             pltpu.VMEM((3, NX, depth, length), f32),
@@ -442,9 +504,17 @@
             dma((slices - 1, spaces - 1)),
             dma((slices - 1, 2)),
             dma((slices - 1, 2)),
+            pltpu.VMEM((2, 4 * half, width), f32),
+            pltpu.VMEM((slices, 2, 4 * half, width), f32),
+            pltpu.VMEM((slices, 4 * rows, width), f32),
+            dma((2,)),
+            dma((2,)),
+            dma((2,)),
+            dma((slices - 1,)),
+            dma((slices - 1,)),
         ],
         compiler_params=pltpu.CompilerParams(
-            collective_id=0, has_side_effects=True, vmem_limit_bytes=48 * 1024 * 1024
+            collective_id=0, has_side_effects=True, vmem_limit_bytes=60 * 1024 * 1024
         ),
     )(starts, labels, coef_table)
 

time: 66.4 us -> 59 us (0.89)
  Pallas kernels: 62.4 us -> 56.5 us
  local copies, waits for them, and re-layouts: 3.83 us -> 2.26 us
    pallas_call x1, Pallas kernels: 62.4 us -> 56.5 us  [shards(): pl.pallas_call(functools.partial(kernel, slices, spaces), out_shape=jax.S...]
    unnamed x7 -> x1, local copies, waits for them, and re-layouts: 3.83 us -> 2.26 us
where the time goes in v2:
time: 59 us; the launch traced here: 58.8 us
  Pallas kernels  56.5 us (96%)
  local copies, waits for them, and re-layouts  2.26 us (4%)
    pallas_call x1, Pallas kernels, shards(): pl.pallas_call(functools.partial(kernel, slices, spaces), out_shape=jax.S...  56.5 us
    unnamed x1, local copies, waits for them, and re-layouts  2.26 us

profile of v2, /device:TPU:0, one launch (start us, length us, event | category | flops | bytes accessed | tf_op | source)
XLA Modules:
  0.0 58.8 jit_solution(221491767954553659)
XLA Ops:
  0.0 56.5 %shard_map.37 = f32[1,4,8,8192]{3,2,1,0:T(8,128)} custom-call(f32[1,4,8,8192]{3,2,1,0:T(8,128)} %starts_hbm.1, s32[8,8192]{1,0:T(8,128)} %labels_hbm.1, f32[3,4]{1,0:T(4,128)} %table_ref.1), custom_call_target="tpu_custom_call" | custom-call | tf_op jit(solution)/shard_map/pallas_call | solution.py:470
  56.5 2.3 %copy.5 = f32[1,4,8,8192]{3,2,1,0:T(8,128)} copy(f32[1,4,8,8192]{3,2,1,0:T(8,128)} %shard_map.37) | data formatting | bytes 2097152

commit v3 on v2

--- a/solution.py
+++ b/solution.py
@@ -146,18 +146,19 @@
     pick_lo = jnp.where(lane // 2 == place, 0.125, 0.0).astype(f32)
     pick_hi = jnp.where(lane // 2 + quarter == place, 0.125, 0.0).astype(f32)
 
-    def restrict(buf, first, count):
+    def restrict(buf, first, count, pairs=half):
         def pair_up(i, carry):
             for c in range(count):
                 both = buf[c, first + 2 * i] + buf[c, first + 2 * i + 1]
-                at = pl.ds(pl.multiple_of((c * half + i) * depth, depth), depth)
+                at = pl.ds(pl.multiple_of((c * pairs + i) * depth, depth), depth)
                 pair_lo[at, :] = both[:, : length // 2]
                 pair_hi[at, :] = both[:, length // 2 :]
             return carry
 
-        lax.fori_loop(0, half, pair_up, 0, unroll=4)
-        even = pl.ds(0, count * rows, stride=2)
-        odd = pl.ds(1, count * rows, stride=2)
+        lax.fori_loop(0, pairs, pair_up, 0, unroll=4)
+        kept = count * pairs * depth // 2
+        even = pl.ds(0, kept, stride=2)
+        odd = pl.ds(1, kept, stride=2)
         low = pair_lo[even, :] + pair_lo[odd, :]
         high = pair_hi[even, :] + pair_hi[odd, :]
         dot = functools.partial(
@@ -254,6 +255,12 @@
     row = lax.broadcasted_iota(jnp.int32, (1, depth, length), 1)
     col = lax.broadcasted_iota(jnp.int32, (1, depth, length), 2)
     gram_copies = None
+    rf_copies = []
+    part_rows = rows // CHUNKS
+
+    def end_state(a):
+        return all_rf[a].reshape(4 * rows, length // 2)
+
     bufs = (field_a, field_b)
     for step in range(FINE):
         src, dst = bufs[step % 2], bufs[(step + 1) % 2]
@@ -295,6 +302,21 @@
             lax.fori_loop(0, span // BLOCK, block, 0)
             if step + 1 < FINE:
                 start_pair(halo_copies(step + 1, chunk, dst))
+            else:
+                piece = pl.ds(chunk * part_rows, part_rows)
+                ends = restrict(dst, 1 + chunk * span, 4, span // 2)
+                all_rf[tm, :, piece, :] = ends.reshape(4, part_rows, length // 2)
+                sent = [
+                    pltpu.make_async_remote_copy(
+                        src_ref=all_rf.at[tm, :, piece, :], dst_ref=all_rf.at[tm, :, piece, :],
+                        send_sem=rf_send.at[off - 1, chunk], recv_sem=rf_recv.at[off - 1, chunk],
+                        device_id={"tm": lax.rem(tm + off, slices)}, device_id_type=MESH,
+                    )
+                    for off in range(1, slices)
+                ]
+                for copy in sent:
+                    copy.start()
+                rf_copies.extend(sent)
         if step == 0:
             wait_pair(edge_pair)
             for copy in edges_copies:
@@ -326,23 +348,6 @@
             lax.fori_loop(0, slices, image_of, 0)
     final = bufs[FINE % 2]
 
-    all_rf[tm] = restrict(final, 1, 4)
-    sibling = tm + 1 - 2 * lax.rem(tm, 2)
-
-    def rf_copy(slot, index, target):
-        return pltpu.make_async_remote_copy(
-            src_ref=all_rf.at[slot], dst_ref=all_rf.at[slot],
-            send_sem=rf_send.at[index], recv_sem=rf_recv.at[index],
-            device_id={"tm": target}, device_id_type=MESH,
-        )
-
-    far = [
-        rf_copy(tm, off - 1, lax.rem(tm + off, slices)) for off in range(2, slices, 2)
-    ]
-    near = [rf_copy(tm, 0, sibling)]
-    for copy in far + near:
-        copy.start()
-
     def total(buf):
         summed = buf[0]
         for s in range(1, spaces):
@@ -371,15 +376,9 @@
                 value = value - factor[a, k] * factor[b, k]
             factor[a, b] = value * inverse[b]
 
-    for off, copy in zip(range(2, slices, 2), far):
+    for copy in rf_copies:
         copy.wait()
-        onward = rf_copy(lax.rem(tm - off + slices, slices), off, sibling)
-        onward.start()
-        near.append(onward)
-    for copy in near:
-        copy.wait()
-
-    defect_ref[...] = all_rf[0] - all_ru[1]
+    defect_ref[...] = end_state(0) - all_ru[1]
     for j in range(1, slices):
         turn = j - 1
         layer_out[turn, 0] = defect_ref[pl.ds(per - 1, layers, stride=per), :]
@@ -403,13 +402,13 @@
             copy.start()
         if j == 1:
             for a in range(slices):
-                images[a] = all_rf[a] - images[a]
+                images[a] = end_state(a) - images[a]
         for c in range(4):
             padded[c, pl.ds(8, rows), :] = defect_ref[pl.ds(c * rows, rows), :]
         wait_pair(pair)
         image = coarse_image(layer_in.at[turn])
         if j + 1 < slices:
-            defect_ref[...] = all_rf[j] - all_ru[j + 1]
+            defect_ref[...] = end_state(j) - all_ru[j + 1]
         for copy in copies:
             copy.wait()
         inner = total(dot_buf.at[turn])
@@ -483,7 +482,7 @@
             pltpu.VMEM((8 * rows, width), f32),
             pltpu.VMEM((3 * rows, width), f32),
             pltpu.VMEM((slices, 4 * rows, width), f32),
-            pltpu.VMEM((slices, 4 * rows, width), f32),
+            pltpu.VMEM((slices, 4, rows, width), f32),
             pltpu.VMEM((spaces, gram_rows, width), f32),
             pltpu.VMEM((slices - 1, spaces, dot_rows, width), f32),
             pltpu.VMEM((4, rows + 16, width), f32),
@@ -496,8 +495,8 @@
             dma((FINE, 2, CHUNKS)),
             dma((slices - 1,)),
             dma((slices - 1,)),
-            dma((slices - 1,)),
-            dma((slices - 1,)),
+            dma((slices - 1, CHUNKS)),
+            dma((slices - 1, CHUNKS)),
             dma((spaces - 1,)),
             dma((spaces - 1,)),
             dma((slices - 1, spaces - 1)),

time: 59 us -> 57.4 us (0.973)
  Pallas kernels: 56.5 us -> 54.9 us
    pallas_call x1, Pallas kernels: 56.5 us -> 54.9 us  [shards(): pl.pallas_call(functools.partial(kernel, slices, spaces), out_shape=jax.S...]
where the time goes in v3:
time: 57.4 us; the launch traced here: 57.2 us
  Pallas kernels  54.9 us (96%)
  local copies, waits for them, and re-layouts  2.26 us (4%)
    pallas_call x1, Pallas kernels, shards(): pl.pallas_call(functools.partial(kernel, slices, spaces), out_shape=jax.S...  54.9 us
    unnamed x1, local copies, waits for them, and re-layouts  2.26 us

profile of v3, /device:TPU:0, one launch (start us, length us, event | category | flops | bytes accessed | tf_op | source)
XLA Modules:
  0.0 57.2 jit_solution(639845637418982320)
XLA Ops:
  0.0 54.9 %shard_map.37 = f32[1,4,8,8192]{3,2,1,0:T(8,128)} custom-call(f32[1,4,8,8192]{3,2,1,0:T(8,128)} %starts_hbm.1, s32[8,8192]{1,0:T(8,128)} %labels_hbm.1, f32[3,4]{1,0:T(4,128)} %table_ref.1), custom_call_target="tpu_custom_call" | custom-call | tf_op jit(solution)/shard_map/pallas_call | solution.py:469
  54.9 2.3 %copy.5 = f32[1,4,8,8192]{3,2,1,0:T(8,128)} copy(f32[1,4,8,8192]{3,2,1,0:T(8,128)} %shard_map.37) | data formatting | bytes 2097152

commit v4 on v3

--- a/solution.py
+++ b/solution.py
@@ -391,7 +391,6 @@
             )
             for way, by in ((0, 1), (1, spaces - 1))
         ]
-        start_pair(pair)
         defect = defect_ref[...]
         for a in range(slices):
             dot_buf[turn, me, pl.ds(a, 1), :] = jnp.sum(all_ru[a] * defect, axis=0, keepdims=True)
@@ -400,6 +399,7 @@
         copies = space_copies(dot_buf.at[turn, me], dot_send.at[turn], dot_recv.at[turn])
         for copy in copies:
             copy.start()
+        start_pair(pair)
         if j == 1:
             for a in range(slices):
                 images[a] = end_state(a) - images[a]

time: 57.4 us -> 56.4 us (0.983)
  Pallas kernels: 54.9 us -> 54 us
    pallas_call x1, Pallas kernels: 54.9 us -> 54 us  [shards(): pl.pallas_call(functools.partial(kernel, slices, spaces), out_shape=jax.S...]
where the time goes in v4:
time: 56.4 us; the launch traced here: 56.2 us
  Pallas kernels  54 us (96%)
  local copies, waits for them, and re-layouts  2.26 us (4%)
    pallas_call x1, Pallas kernels, shards(): pl.pallas_call(functools.partial(kernel, slices, spaces), out_shape=jax.S...  54 us
    unnamed x1, local copies, waits for them, and re-layouts  2.26 us

profile of v4, /device:TPU:0, one launch (start us, length us, event | category | flops | bytes accessed | tf_op | source)
XLA Modules:
  0.0 56.2 jit_solution(11973428881284680504)
XLA Ops:
  0.0 54.0 %shard_map.37 = f32[1,4,8,8192]{3,2,1,0:T(8,128)} custom-call(f32[1,4,8,8192]{3,2,1,0:T(8,128)} %starts_hbm.1, s32[8,8192]{1,0:T(8,128)} %labels_hbm.1, f32[3,4]{1,0:T(4,128)} %table_ref.1), custom_call_target="tpu_custom_call" | custom-call | tf_op jit(solution)/shard_map/pallas_call | solution.py:469
  54.0 2.3 %copy.5 = f32[1,4,8,8192]{3,2,1,0:T(8,128)} copy(f32[1,4,8,8192]{3,2,1,0:T(8,128)} %shard_map.37) | data formatting | bytes 2097152

commit v5 on v4

--- a/solution.py
+++ b/solution.py
@@ -183,7 +183,7 @@
                 send_sem=sends.at[off - 1], recv_sem=recvs.at[off - 1],
                 device_id={"space": lax.rem(me + off, spaces)}, device_id_type=MESH,
             )
-            for off in range(1, spaces)
+            for off in sorted(range(1, spaces), key=lambda off: abs(2 * off - spaces))
         ]
 
     per = depth // 2

time: 56.4 us -> 56.8 us (level)
  no operation moved by 1% of the time
where the time goes in v5:
time: 56.8 us; the launch traced here: 56.6 us
  Pallas kernels  54.3 us (96%)
  local copies, waits for them, and re-layouts  2.26 us (4%)
    pallas_call x1, Pallas kernels, shards(): pl.pallas_call(functools.partial(kernel, slices, spaces), out_shape=jax.S...  54.3 us
    unnamed x1, local copies, waits for them, and re-layouts  2.26 us

profile of v5, /device:TPU:0, one launch (start us, length us, event | category | flops | bytes accessed | tf_op | source)
XLA Modules:
  0.0 56.6 jit_solution(6122984419208712060)
XLA Ops:
  0.0 54.3 %shard_map.37 = f32[1,4,8,8192]{3,2,1,0:T(8,128)} custom-call(f32[1,4,8,8192]{3,2,1,0:T(8,128)} %starts_hbm.1, s32[8,8192]{1,0:T(8,128)} %labels_hbm.1, f32[3,4]{1,0:T(4,128)} %table_ref.1), custom_call_target="tpu_custom_call" | custom-call | tf_op jit(solution)/shard_map/pallas_call | solution.py:469
  54.3 2.3 %copy.5 = f32[1,4,8,8192]{3,2,1,0:T(8,128)} copy(f32[1,4,8,8192]{3,2,1,0:T(8,128)} %shard_map.37) | data formatting | bytes 2097152
